TPU v7x, 32 devices: a whole 2x2x4 slice. The times are simulated.
32 devices in a mesh: group: 2 (over y), wide: 4 (over x, core), narrow: 4 (over z).
Axes of the slice: x: 2, y: 2, z: 4, core: 2. Of those that a mesh axis runs over, the one named last changes fastest.
Arguments:
- query_factor: bfloat16 [4, 128, 1536, 128], P('group', 'narrow', 'wide'), parts along dimension 0, may hold values from -6 to 6
- latent_factor: bfloat16 [4, 128, 512, 128], P('group', 'narrow', 'wide'), parts along dimension 0, may hold values from -6 to 6
- head_owner: int32 [4, 128], P('group'), parts along dimension 0, may hold values from 0 to 3, as said below
Outputs:
- absorbed_owned: bfloat16 [4, 256, 1536, 512], P('group', 'narrow', 'wide'), parts along dimension 0
There are 2 independent parts, one for each index of `group`. A program takes and returns all parts, laid end to end along the dimension named above; each array names one. Nothing has to cross between parts.
Inputs may be any that keep to these rules, and one draw needn't show every extreme that they name: `head_owner`: in each layer, at most 16 of the 32 heads of each aligned block of heads (heads k * 32 to (k + 1) * 32 - 1) have one owner, and some owner takes exactly 16 from every block, so holds 64 heads.
All inputs are finite; a program needn't handle non-finite values.
Results may differ from a plain program's by a relative error of at most 0.001.
Values may be sent and summed in bfloat16 or wider, within the bound.
A program may use at most 192 MiB of HBM per device.

v0:
```python
import jax
import jax.numpy as jnp
from jax import lax
from jax.sharding import PartitionSpec as P

qk_scale = 192.0 ** (-0.5)


def absorb(query_part, piece):
    product = jnp.einsum("lhqd,lhkd->lhqk", query_part, piece, preferred_element_type=jnp.float32)
    return (product * qk_scale).astype(jnp.bfloat16)


def bucket_matrix(local_owner, peers, bucket):
    onehot = (local_owner[:, :, None] == jnp.arange(peers, dtype=jnp.int32)[None, None, :]).astype(
        jnp.int32
    )
    before = jnp.cumsum(onehot, axis=1) - onehot
    target = local_owner * bucket + jnp.sum(before * onehot, axis=2)
    targets = jnp.arange(peers * bucket, dtype=jnp.int32)
    return (target[:, None, :] == targets[None, :, None]).astype(jnp.bfloat16)


def collect_matrix(head_owner, own_index, peers, bucket):
    layers = head_owner.shape[0]
    blocks = head_owner.reshape(layers, peers, -1)
    counts = jnp.sum((blocks == own_index).astype(jnp.int32), axis=2)
    offset = jnp.cumsum(counts, axis=1) - counts
    within = jnp.arange(bucket, dtype=jnp.int32)
    is_live = within[None, None, :] < counts[:, :, None]
    target = jnp.where(is_live, offset[:, :, None] + within[None, None, :], -1).reshape(
        layers, peers * bucket
    )
    slot_rows = jnp.arange(peers * bucket, dtype=jnp.int32)
    return (slot_rows[None, :, None] == target[:, None, :]).astype(jnp.bfloat16)


def on_device(query_factor, latent_factor, head_owner):
    peers = lax.axis_size("narrow")
    own_index = lax.axis_index("narrow")
    heads_total = head_owner.shape[1]
    bucket = 2 * heads_total // (peers * peers)
    per_device = query_factor.shape[1]
    local_owner = lax.dynamic_slice_in_dim(head_owner, own_index * per_device, per_device, 1)
    spread = bucket_matrix(local_owner, peers, bucket)
    collect = collect_matrix(head_owner, own_index, peers, bucket)
    sent_query = jnp.einsum(
        "lrh,lhqd->lrqd", spread, query_factor, preferred_element_type=jnp.float32
    ).astype(jnp.bfloat16)
    sent_latent = jnp.einsum(
        "lrh,lhkd->lrkd", spread, latent_factor, preferred_element_type=jnp.float32
    ).astype(jnp.bfloat16)
    got_query, got_latent = (
        lax.all_to_all(sent_query, "narrow", split_axis=1, concat_axis=1, tiled=True),
        lax.all_to_all(sent_latent, "narrow", split_axis=1, concat_axis=1, tiled=True),
    )
    own_query = jnp.einsum(
        "ltr,lrqd->ltqd", collect, got_query, preferred_element_type=jnp.float32
    ).astype(jnp.bfloat16)
    own_latent = jnp.einsum(
        "ltr,lrkd->ltkd", collect, got_latent, preferred_element_type=jnp.float32
    ).astype(jnp.bfloat16)
    result = absorb(own_query, lax.all_gather(own_latent, "wide", axis=2, tiled=True))
    return result


def solution(mesh):
    in_specs = (
        P("group", "narrow", "wide", None),
        P("group", "narrow", "wide", None),
        P("group", None),
    )
    out_specs = P("group", "narrow", "wide", None)
    return jax.shard_map(
        on_device, mesh=mesh, in_specs=in_specs, out_specs=out_specs, check_vma=False
    )
```

profile of v0, /device:TPU:12, one launch (start us, length us, event | category | flops | bytes accessed | tf_op | source)
XLA Modules:
  0.0 522.6 jit_solution(5205504015396354224)
XLA Ops:
  6.5 0.0 copy-start
  6.5 0.0 copy-start.2
  6.5 0.9 constant_dynamic-slice_fusion
  7.4 0.1 fusion.16
  7.5 0.1 reduce_window_sum.23
  7.6 0.2 select_reduce_fusion
  7.8 0.8 multiply_add_fusion
  8.5 0.0 copy-done
  8.5 1.7 fusion.6
  10.3 4.7 copy.29
  15.0 5.3 %all-to-all-start.1 = ((bf16[2,64,128,128]{3,2,0,1:T(8,128)(2,1)}), bf16[2,64,128,128]{3,2,0,1:T(8,128)(2,1)}, u32[]{:S(2)}, u32[]{:S(2)}) async-start(bf16[2,64,128,128]{3,2,0,1:T(8,128)(2,1)} %copy.29), calls=%async_computation.1 | async-start | bytes 8388608 | tf_op jit(solution)/shard_map/all_to_all | solution.py:55
  20.3 0.0 all-gather.2.cloned.1.call-start
  20.3 0.1 lt.33
  20.4 0.0 copy-done.2
  20.4 0.1 reshape.46
  20.5 0.1 reduce_sum.18
  20.6 0.2 reduce_window_sum.22
  20.8 0.1 lt.35
  20.8 0.1 lt.36
  20.9 0.1 add.23
  21.0 0.1 add.24
  21.1 89.3 %all-to-all-done.1 = bf16[2,64,128,128]{3,2,0,1:T(8,128)(2,1)} async-done(((bf16[2,64,128,128]{3,2,0,1:T(8,128)(2,1)}), bf16[2,64,128,128]{3,2,0,1:T(8,128)(2,1)}, u32[]{:S(2)}, u32[]{:S(2)}) %all-to-all-start.1) | async-done | bytes 4194336 | tf_op jit(solution)/shard_map/all_to_all | solution.py:55
  110.4 5.7 %fusion.4 = bf16[2,64,128,128]{3,1,2,0:T(8,128)(2,1)S(1)} fusion(bf16[2,64,128,128]{3,2,0,1:T(8,128)(2,1)} %all-to-all-done.1, s32[2,64]{1,0:T(2,128)S(1)} %compare_select_fusion), kind=kOutput, calls=%fused_computation.9 | convolution fusion | flops 268443648 | bytes 8389120 | tf_op jit(solution)/shard_map/ltr,lrkd->ltkd/dot_general | solution.py:60
  116.0 4.7 copy.28
  120.8 0.0 all-gather.2.cloned.1.call-update
  120.8 11.1 %fusion.2 = bf16[2,64,384,128]{3,1,2,0:T(8,128)(2,1)S(1)} fusion(bf16[2,32,384,128]{3,2,1,0:T(8,128)(2,1)} %param.3, s32[2,32]{1,0:T(2,128)S(1)} %multiply_add_fusion), kind=kOutput, calls=%fused_computation.7 | convolution fusion | flops 402657280 | bytes 18874624 | tf_op jit(solution)/shard_map/lrh,lhqd->lrqd/dot_general | solution.py:47
  131.9 27.3 %copy.27 = bf16[2,64,384,128]{3,2,0,1:T(8,128)(2,1)S(1)} copy(bf16[2,64,384,128]{3,1,2,0:T(8,128)(2,1)S(1)} %fusion.2) | data formatting | bytes 25165824 | tf_op jit(solution)/shard_map/lrh,lhqd->lrqd/dot_general | solution.py:47
  159.2 278.6 %all_to_all.10 = bf16[2,64,384,128]{3,2,0,1:T(8,128)(2,1)} all-to-all(bf16[2,64,384,128]{3,2,0,1:T(8,128)(2,1)S(1)} %copy.27), channel_id=1, replica_groups=mesh['group'=2,'wide'=4,'narrow'=4] {'narrow'}, dimensions={1} | all-to-all | bytes 25165824 | tf_op jit(solution)/shard_map/all_to_all | solution.py:54
  437.7 17.6 %fusion = bf16[2,64,384,128]{3,1,2,0:T(8,128)(2,1)} fusion(bf16[2,64,384,128]{3,2,0,1:T(8,128)(2,1)} %all_to_all.10, s32[2,64]{1,0:T(2,128)S(1)} %compare_select_fusion), kind=kOutput, calls=%fused_computation.3 | convolution fusion | flops 805314560 | bytes 25166336 | tf_op jit(solution)/shard_map/ltr,lrqd->ltqd/dot_general | solution.py:57
  455.4 0.0 all-gather.2.cloned.1.call-done
  455.4 60.4 %multiply_convert_fusion = bf16[2,64,384,512]{3,2,1,0:T(8,128)(2,1)} fusion(bf16[2,64,512,128]{3,2,1,0:T(8,128)(2,1)} %all-gather.2.cloned.1.call-done, bf16[2,64,384,128]{3,1,2,0:T(8,128)(2,1)} %fusion), kind=kOutput, calls=%fused_computation | convolution fusion | flops 6492782592 | bytes 79691776 | tf_op jit(solution)/shard_map/lhqd,lhkd->lhqk/dot_general | solution.py:10
  515.8 0.0 copy-done.1
  (5 shorter events, 0.0 us)
Async XLA Ops:
  6.5 2.0 copy-start
  6.5 13.8 %copy-start.2 = (s32[2,128]{1,0:T(2,128)S(1)}, s32[2,128]{1,0:T(2,128)}, u32[]{:S(2)}) copy-start(s32[2,128]{1,0:T(2,128)} %param.5) | copy-start | bytes 3076
  15.0 95.4 %all-to-all-start.1 = ((bf16[2,64,128,128]{3,2,0,1:T(8,128)(2,1)}), bf16[2,64,128,128]{3,2,0,1:T(8,128)(2,1)}, u32[]{:S(2)}, u32[]{:S(2)}) async-start(bf16[2,64,128,128]{3,2,0,1:T(8,128)(2,1)} %copy.29), calls=%async_computation.1 | async-start | bytes 8388608 | tf_op jit(solution)/shard_map/all_to_all | solution.py:55
  20.3 435.1 %all-gather.2.cloned.1.call-start = ((), (), s32[]{:S(2)}) async-start(), calls=%async_computation.2 | async-start | bytes 20971520 | tf_op jit(solution)/shard_map/all_gather | solution.py:63
  455.4 60.4 %copy-start.1 = (bf16[2,32,128,128]{3,2,1,0:T(8,128)(2,1)S(1)}, bf16[2,32,128,128]{3,2,1,0:T(8,128)(2,1)}, u32[]{:S(2)}) copy-start(bf16[2,32,128,128]{3,2,1,0:T(8,128)(2,1)} %param.4) | copy-start | bytes 6291460
Sparse Core Ops, SparseCore 0:
  120.9 107.8 all-gather.1
where the time goes:
time: 526 us; the launch traced here: 523 us
  blocking collectives  279 us (53%)
  matrix products  96.5 us (18%)
  waiting for transfers between devices  89.3 us (17%)
  local copies, waits for them, and re-layouts  38.1 us (7%)
  between operations  13.4 us (3%)
  starting transfers between devices  5.31 us (1%)
    all_to_all x1, blocking collectives, on_device(): lax.all_to_all(sent_query, 'narrow', split_axis=1, concat_axis=1, tiled=T...  279 us
    all_to_all x1, waiting for transfers between devices, on_device(): lax.all_to_all(sent_latent, 'narrow', split_axis=1, concat_axis=1, tiled=...  89.3 us
    dot_general x1, matrix products, absorb(): jnp.einsum('lhqd,lhkd->lhqk', query_part, piece, preferred_element_type=j...  60.4 us
    dot_general x1, local copies, waits for them, and re-layouts, on_device(): jnp.einsum('lrh,lhqd->lrqd', spread, query_factor, preferred_element_type...  27.3 us
    dot_general x1, matrix products, on_device(): jnp.einsum('ltr,lrqd->ltqd', collect, got_query, preferred_element_type=j...  17.6 us
    dot_general x1, matrix products, on_device(): jnp.einsum('lrh,lhqd->lrqd', spread, query_factor, preferred_element_type...  11.1 us
  transfers between devices with their start and end apart: 2, of which 1 were waited for; matrix products, arithmetic and copies ran while one was open for 11% of the time, Pallas kernels for 0%

commit v1 on v0

v1 whole, which is shorter than its diff:
```python
import functools

import jax
import jax.numpy as jnp
from jax import lax
from jax.experimental import pallas as pl
from jax.experimental.pallas import tpu as pltpu
from jax.sharding import PartitionSpec as P

qk_scale = 192.0 ** (-0.5)
MESH = pl.DeviceIdType.MESH


def send_rows(local_owner, bucket):
    heads = local_owner.shape[1]
    same = local_owner[:, :, None] == local_owner[:, None, :]
    earlier = jnp.arange(heads)[None, :, None] > jnp.arange(heads)[None, None, :]
    rank = jnp.sum((same & earlier).astype(jnp.int32), axis=2)
    return local_owner * bucket + rank


def slot_sources(head_owner, own_index, peers, bucket):
    layers = head_owner.shape[0]
    counts = jnp.sum((head_owner.reshape(layers, peers, -1) == own_index).astype(jnp.int32), axis=2)
    upto = jnp.arange(peers)[:, None] >= jnp.arange(peers)[None, :]
    ends = jnp.sum(jnp.where(upto[None], counts[:, None, :], 0), axis=2)
    starts = ends - counts
    slots = jnp.arange(peers * bucket, dtype=jnp.int32)[None, :, None]
    held = (slots >= starts[:, None, :]) & (slots < ends[:, None, :])
    rows = jnp.arange(peers, dtype=jnp.int32)[None, None, :] * bucket + slots - starts[:, None, :]
    source = jnp.sum(jnp.where(held, rows, 0), axis=2)
    source = source + (jnp.arange(layers, dtype=jnp.int32) * (peers * bucket))[:, None]
    live = jnp.any(held, axis=2).astype(jnp.int32)
    return source.reshape(-1), live.reshape(-1)


def pack_kernel(rows_ref, query_ref, latent_ref, sent_query_ref, sent_latent_ref, sems):
    layers, heads = query_ref.shape[:2]

    @pl.loop(0, layers * heads)
    def _(i):
        layer, head = i // heads, i % heads
        row = rows_ref[i]
        pltpu.make_async_copy(latent_ref.at[layer, head], sent_latent_ref.at[layer, row], sems.at[0]).start()
        pltpu.make_async_copy(query_ref.at[layer, head], sent_query_ref.at[layer, row], sems.at[1]).start()

    pltpu.make_async_copy(latent_ref, latent_ref, sems.at[0]).wait()
    pltpu.make_async_copy(query_ref, query_ref, sems.at[1]).wait()


def pack(rows, query_factor, latent_factor, width):
    layers = query_factor.shape[0]
    return pl.pallas_call(
        pack_kernel,
        out_shape=(
            jax.ShapeDtypeStruct((layers, width) + query_factor.shape[2:], jnp.bfloat16),
            jax.ShapeDtypeStruct((layers, width) + latent_factor.shape[2:], jnp.bfloat16),
        ),
        grid_spec=pltpu.PrefetchScalarGridSpec(
            num_scalar_prefetch=1,
            grid=(),
            in_specs=[pl.BlockSpec(memory_space=pl.ANY)] * 2,
            out_specs=(pl.BlockSpec(memory_space=pl.ANY),) * 2,
            scratch_shapes=[pltpu.SemaphoreType.DMA((2,))],
        ),
    )(rows.reshape(-1), query_factor, latent_factor)


def exchange_kernel(
    peers, wides, bucket, sent_query_ref, sent_latent_ref, got_query_ref, got_latent_ref,
    query_send, query_recv, latent_send, latent_recv, wide_send, wide_recv, local_sem,
):
    group, wide, me = lax.axis_index("group"), lax.axis_index("wide"), lax.axis_index("narrow")
    layers = sent_query_ref.shape[0]
    part = sent_latent_ref.shape[2]

    def at_narrow(other):
        return (group, wide, other)

    def at_wide(step):
        return (group, lax.rem(wide + step, wides), me)

    barrier = pltpu.get_barrier_semaphore()
    for k in range(1, peers):
        pl.semaphore_signal(barrier, inc=1, device_id=at_narrow(lax.rem(me + k, peers)), device_id_type=MESH)

    @pl.loop(1, wides)
    def _(step):
        pl.semaphore_signal(barrier, inc=1, device_id=at_wide(step), device_id_type=MESH)

    pl.semaphore_wait(barrier, peers - 1 + wides - 1)

    def heads_of(peer):
        return pl.ds(pl.multiple_of(peer * bucket, bucket), bucket)

    def part_of(index):
        return pl.ds(pl.multiple_of(index * part, part), part)

    def narrow_query(layer, k):
        other = lax.rem(me + k, peers)
        return pltpu.make_async_remote_copy(
            src_ref=sent_query_ref.at[layer, heads_of(other)],
            dst_ref=got_query_ref.at[layer, heads_of(me)],
            send_sem=query_send.at[layer, k],
            recv_sem=query_recv.at[layer, k],
            device_id=at_narrow(other),
            device_id_type=MESH,
        )

    def narrow_latent(layer, k):
        other = lax.rem(me + k, peers)
        return pltpu.make_async_remote_copy(
            src_ref=sent_latent_ref.at[layer, heads_of(other)],
            dst_ref=got_latent_ref.at[layer, heads_of(me), part_of(wide)],
            send_sem=latent_send.at[layer, k],
            recv_sem=latent_recv.at[layer, k],
            device_id=at_narrow(other),
            device_id_type=MESH,
        )

    def wide_latent(layer, k, step):
        origin = lax.rem(me + peers - k, peers)
        landed = got_latent_ref.at[layer, heads_of(origin), part_of(wide)]
        return pltpu.make_async_remote_copy(
            src_ref=sent_latent_ref.at[layer, heads_of(me)] if k == 0 else landed,
            dst_ref=landed,
            send_sem=wide_send.at[layer, k, step],
            recv_sem=wide_recv.at[layer, k, step],
            device_id=at_wide(step),
            device_id_type=MESH,
        )

    def own_query(layer):
        return pltpu.make_async_copy(
            sent_query_ref.at[layer, heads_of(me)], got_query_ref.at[layer, heads_of(me)], local_sem.at[0, layer]
        )

    def own_latent(layer):
        return pltpu.make_async_copy(
            sent_latent_ref.at[layer, heads_of(me)],
            got_latent_ref.at[layer, heads_of(me), part_of(wide)],
            local_sem.at[1, layer],
        )

    for layer in range(layers):
        for k in range(1, peers):
            narrow_latent(layer, k).start()
    for layer in range(layers):
        for k in range(1, peers):
            narrow_query(layer, k).start()
    for layer in range(layers):
        own_query(layer).start()
        own_latent(layer).start()
        pl.loop(1, wides)(lambda step: wide_latent(layer, 0, step).start())
    for layer in range(layers):
        for k in range(1, peers):
            narrow_latent(layer, k).wait_recv()
            pl.loop(1, wides)(lambda step: wide_latent(layer, k, step).start())
    for layer in range(layers):
        for k in range(peers):
            pl.loop(1, wides)(lambda step: wide_latent(layer, k, step).wait())
    for layer in range(layers):
        own_query(layer).wait()
        own_latent(layer).wait()
        for k in range(1, peers):
            narrow_latent(layer, k).wait_send()
            narrow_query(layer, k).wait()


def exchange(sent_query, sent_latent, peers, wides, bucket):
    layers, width, part, depth = sent_latent.shape
    dma = pltpu.SemaphoreType.DMA
    return pl.pallas_call(
        functools.partial(exchange_kernel, peers, wides, bucket),
        out_shape=(
            jax.ShapeDtypeStruct(sent_query.shape, jnp.bfloat16),
            jax.ShapeDtypeStruct((layers, width, wides * part, depth), jnp.bfloat16),
        ),
        in_specs=[pl.BlockSpec(memory_space=pl.ANY)] * 2,
        out_specs=(pl.BlockSpec(memory_space=pl.ANY),) * 2,
        scratch_shapes=[
            dma((layers, peers)), dma((layers, peers)),
            dma((layers, peers)), dma((layers, peers)),
            dma((layers, peers, wides)), dma((layers, peers, wides)),
            dma((2, layers)),
        ],
        compiler_params=pltpu.CompilerParams(collective_id=0, has_side_effects=True),
    )(sent_query, sent_latent)


def absorb_kernel(each, source_ref, live_ref, *refs):
    queries, latents, out_ref = refs[:each], refs[each:2 * each], refs[2 * each]
    first = pl.program_id(0) * each
    for b in range(each):
        product = lax.dot_general(
            queries[b][0], latents[b][0], (((1,), (1,)), ((), ())), preferred_element_type=jnp.float32
        )
        taken = live_ref[first + b] > 0
        out_ref[b] = jnp.where(taken, product * qk_scale, 0.0).astype(jnp.bfloat16)


def absorb(source, live, got_query, got_latent):
    layers, width, rows, depth = got_query.shape
    columns = got_latent.shape[2]
    slots = layers * width
    each = 4

    def spec(b, size):
        return pl.BlockSpec((1, size, depth), lambda i, source_ref, live_ref: (source_ref[i * each + b], 0, 0))

    query = got_query.reshape(slots, rows, depth)
    latent = got_latent.reshape(slots, columns, depth)
    result = pl.pallas_call(
        functools.partial(absorb_kernel, each),
        out_shape=jax.ShapeDtypeStruct((slots, rows, columns), jnp.bfloat16),
        grid_spec=pltpu.PrefetchScalarGridSpec(
            num_scalar_prefetch=2,
            grid=(slots // each,),
            in_specs=[spec(b, rows) for b in range(each)] + [spec(b, columns) for b in range(each)],
            out_specs=pl.BlockSpec((each, rows, columns), lambda i, source_ref, live_ref: (i, 0, 0)),
        ),
        compiler_params=pltpu.CompilerParams(vmem_limit_bytes=40 * 1024 * 1024),
    )(source, live, *([query] * each), *([latent] * each))
    return result.reshape(layers, width, rows, columns)


def on_device(query_factor, latent_factor, head_owner):
    peers, wides = lax.axis_size("narrow"), lax.axis_size("wide")
    own_index = lax.axis_index("narrow")
    heads_total = head_owner.shape[1]
    bucket = 2 * heads_total // (peers * peers)
    per_device = query_factor.shape[1]
    local_owner = lax.dynamic_slice_in_dim(head_owner, own_index * per_device, per_device, 1)
    rows = send_rows(local_owner, bucket)
    source, live = slot_sources(head_owner, own_index, peers, bucket)
    sent_query, sent_latent = pack(rows, query_factor, latent_factor, peers * bucket)
    got_query, got_latent = exchange(sent_query, sent_latent, peers, wides, bucket)
    return absorb(source, live, got_query, got_latent)


def solution(mesh):
    in_specs = (
        P("group", "narrow", "wide", None),
        P("group", "narrow", "wide", None),
        P("group", None),
    )
    out_specs = P("group", "narrow", "wide", None)
    return jax.shard_map(
        on_device, mesh=mesh, in_specs=in_specs, out_specs=out_specs, check_vma=False
    )
```

time: 526 us -> 666 us (1.27)
  Pallas kernels: 0 us -> 657 us
  blocking collectives: 279 us -> 0 us
  matrix products: 96.5 us -> 0 us
  waiting for transfers between devices: 89.3 us -> 0 us
  local copies, waits for them, and re-layouts: 38.1 us -> 6.25 us
  between operations: 13.4 us -> 0.05 us
    pallas_call x0 -> x3, Pallas kernels: none -> 657 us  [the longest x1 365 us: exchange(): pl.pallas_call(functools.partial(exchange_kernel, peers, wides, bucket),...]
    all_to_all x1 -> x0, blocking collectives: 279 us -> none  [on_device(): lax.all_to_all(sent_query, 'narrow', split_axis=1, concat_axis=1, tiled=T...]
    dot_general x5 -> x0, matrix products: 96.5 us -> none  [the longest x1 60.4 us: absorb(): jnp.einsum('lhqd,lhkd->lhqk', query_part, piece, preferred_element_type=j...]
    all_to_all x1 -> x0, waiting for transfers between devices: 89.3 us -> none  [on_device(): lax.all_to_all(sent_latent, 'narrow', split_axis=1, concat_axis=1, tiled=...]
    dot_general x3 -> x0, local copies, waits for them, and re-layouts: 36.7 us -> none  [the longest x1 27.3 us: on_device(): jnp.einsum('lrh,lhqd->lrqd', spread, query_factor, preferred_element_type...]
  transfers between devices with their start and end apart: 2 -> 0, of which waited for: 1 -> 0; matrix products, arithmetic and copies ran while one was open for 11% -> 0% of each run, Pallas kernels for 0% -> 0%
where the time goes in v1:
time: 666 us
  Pallas kernels  657 us (99%)
    pallas_call x1, Pallas kernels, exchange(): pl.pallas_call(functools.partial(exchange_kernel, peers, wides, bucket),...  365 us
    pallas_call x1, Pallas kernels, pack(): pl.pallas_call(pack_kernel, out_shape=(jax.ShapeDtypeStruct((layers, widt...  256 us
    pallas_call x1, Pallas kernels, absorb(): pl.pallas_call(functools.partial(absorb_kernel, each), out_shape=jax.Shap...  36.3 us

profile of v1, /device:TPU:12, one launch (start us, length us, event | category | flops | bytes accessed | tf_op | source)
XLA Modules:
  0.0 665.9 jit_solution(143683134509201387)
XLA Ops:
  0.0 0.7 compare_convert_fusion
  0.7 0.8 constant_dynamic-slice_fusion
  1.5 0.1 iota_add_fusion
  1.5 0.1 reshape.95
  1.6 0.1 reduce_sum.36
  1.7 0.2 select_reduce_fusion.1
  1.9 0.1 select_reduce_fusion
  2.0 0.1 fusion.1
  2.1 0.1 broadcast_add_fusion
  2.1 0.1 add.41.source_ref
  2.2 0.1 reshape.96.live_ref
  2.3 0.2 convert_reduce_fusion
  2.5 0.8 multiply_add_fusion
  3.3 0.7 reshape.91.rows_ref
  3.9 255.9 %shard_map.37 = (bf16[2,64,384,128]{3,2,1,0:T(8,128)(2,1)}, bf16[2,64,128,128]{3,2,1,0:T(8,128)(2,1)}) custom-call(s32[64]{0:T(128)} %reshape.91.rows_ref, bf16[2,32,384,128]{3,2,1,0:T(8,128)(2,1)} %query_ref.1, bf16[2,32,128,128]{3,2,1,0:T(8,128)(2,1)} %latent_ref.1), custom_call_target="tpu_custom_call" | custom-call | tf_op jit(solution)/shard_map/pallas_call | solution.py:53
  259.8 365.1 %shard_map.38 = (bf16[2,64,384,128]{3,2,1,0:T(8,128)(2,1)}, bf16[2,64,512,128]{3,2,1,0:T(8,128)(2,1)}) custom-call(bf16[2,64,384,128]{3,2,1,0:T(8,128)(2,1)} %get-tuple-element.9.sent_query_ref, bf16[2,64,128,128]{3,2,1,0:T(8,128)(2,1)} %get-tuple-element.10.sent_latent_ref), custom_call_target="tpu_custom_call" | custom-call | tf_op jit(solution)/shard_map/pallas_call | solution.py:173
  625.0 0.0 copy-start
  625.0 4.6 copy-done
  629.5 36.3 %shard_map.39 = bf16[128,384,512]{2,1,0:T(8,128)(2,1)} custom-call(s32[128]{0:T(128)S(1)} %add.41.source_ref, s32[128]{0:T(128)S(1)} %reshape.96.live_ref, bf16[128,384,128]{2,1,0:T(8,128)(2,1)S(1)} %bitcast.3, bf16[128,384,128]{2,1,0:T(8,128)(2,1)S(1)} %bitcast.4, bf16[128,384,128]{2,1,0:T(8,128)(2,1)S(1)} %bitcast.5, bf16[128,384,128]{2,1,0:T(8,128)(2,1)S(1)} %bitcast.6, ...), custom_call_target="tpu_custom_call" | custom-call | tf_op jit(solution)/shard_map/pallas_call | solution.py:213
  (6 shorter events, 0.0 us)
Async XLA Ops:
  625.0 4.6 copy-start

commit v2 on v1

--- a/solution.py
+++ b/solution.py
@@ -34,15 +34,29 @@
     return source.reshape(-1), live.reshape(-1)
 
 
-def pack_kernel(rows_ref, query_ref, latent_ref, sent_query_ref, sent_latent_ref, sems):
+def pack_kernel(rows_ref, query_ref, latent_ref, sent_query_ref, sent_latent_ref, query_vmem, latent_vmem, in_sems, sems):
     layers, heads = query_ref.shape[:2]
-
-    @pl.loop(0, layers * heads)
-    def _(i):
-        layer, head = i // heads, i % heads
-        row = rows_ref[i]
-        pltpu.make_async_copy(latent_ref.at[layer, head], sent_latent_ref.at[layer, row], sems.at[0]).start()
-        pltpu.make_async_copy(query_ref.at[layer, head], sent_query_ref.at[layer, row], sems.at[1]).start()
+    pieces = 4
+    each = heads // pieces
+
+    def read(ref, vmem, which, layer, piece):
+        part = pl.ds(piece * each, each)
+        return pltpu.make_async_copy(ref.at[layer, part], vmem.at[layer, part], in_sems.at[which, layer, piece])
+
+    for layer in range(layers):
+        for piece in range(pieces):
+            read(latent_ref, latent_vmem, 0, layer, piece).start()
+            read(query_ref, query_vmem, 1, layer, piece).start()
+    for layer in range(layers):
+        for piece in range(pieces):
+            read(latent_ref, latent_vmem, 0, layer, piece).wait()
+            read(query_ref, query_vmem, 1, layer, piece).wait()
+
+            @pl.loop(piece * each, (piece + 1) * each)
+            def _(head):
+                row = rows_ref[layer * heads + head]
+                pltpu.make_async_copy(latent_vmem.at[layer, head], sent_latent_ref.at[layer, row], sems.at[0]).start()
+                pltpu.make_async_copy(query_vmem.at[layer, head], sent_query_ref.at[layer, row], sems.at[1]).start()
 
     pltpu.make_async_copy(latent_ref, latent_ref, sems.at[0]).wait()
     pltpu.make_async_copy(query_ref, query_ref, sems.at[1]).wait()
@@ -61,8 +75,14 @@
             grid=(),
             in_specs=[pl.BlockSpec(memory_space=pl.ANY)] * 2,
             out_specs=(pl.BlockSpec(memory_space=pl.ANY),) * 2,
-            scratch_shapes=[pltpu.SemaphoreType.DMA((2,))],
-        ),
+            scratch_shapes=[
+                pltpu.VMEM(query_factor.shape, jnp.bfloat16),
+                pltpu.VMEM(latent_factor.shape, jnp.bfloat16),
+                pltpu.SemaphoreType.DMA((2, layers, 4)),
+                pltpu.SemaphoreType.DMA((2,)),
+            ],
+        ),
+        compiler_params=pltpu.CompilerParams(vmem_limit_bytes=40 * 1024 * 1024),
     )(rows.reshape(-1), query_factor, latent_factor)
 
 
@@ -203,7 +223,7 @@
     layers, width, rows, depth = got_query.shape
     columns = got_latent.shape[2]
     slots = layers * width
-    each = 4
+    each = 8
 
     def spec(b, size):
         return pl.BlockSpec((1, size, depth), lambda i, source_ref, live_ref: (source_ref[i * each + b], 0, 0))

time: 666 us -> 412 us (0.62)
  Pallas kernels: 657 us -> 397 us
    pallas_call x1, Pallas kernels: 256 us -> 5.26 us  [pack(): pl.pallas_call(pack_kernel, out_shape=(jax.ShapeDtypeStruct((layers, widt...]
    pallas_call x1, Pallas kernels: 36.3 us -> 26.7 us  [absorb(): pl.pallas_call(functools.partial(absorb_kernel, each), out_shape=jax.Shap...]
where the time goes in v2:
time: 412 us; the launch traced here: 411 us
  Pallas kernels  397 us (96%)
  local copies, waits for them, and re-layouts  12 us (3%)
    pallas_call x1, Pallas kernels, exchange(): pl.pallas_call(functools.partial(exchange_kernel, peers, wides, bucket),...  365 us
    pallas_call x1, Pallas kernels, absorb(): pl.pallas_call(functools.partial(absorb_kernel, each), out_shape=jax.Shap...  26.7 us
    unnamed x8, local copies, waits for them, and re-layouts  10.9 us

profile of v2, /device:TPU:12, one launch (start us, length us, event | category | flops | bytes accessed | tf_op | source)
XLA Modules:
  0.0 411.3 jit_solution(13834870702794000645)
XLA Ops:
  0.0 0.7 compare_convert_fusion
  0.7 0.8 constant_dynamic-slice_fusion
  1.5 0.1 iota_add_fusion
  1.5 0.1 reshape.95
  1.6 0.1 reduce_sum.36
  1.7 0.2 select_reduce_fusion.1
  1.9 0.1 select_reduce_fusion
  2.0 0.1 fusion.1
  2.1 0.1 broadcast_add_fusion
  2.1 0.1 add.41.source_ref
  2.2 0.1 reshape.96.live_ref
  2.3 0.2 convert_reduce_fusion
  2.5 0.8 multiply_add_fusion
  3.3 0.1 reshape.91.rows_ref
  3.3 0.0 copy-start.1
  3.4 2.8 copy-done.1
  6.1 0.0 copy-start.3
  6.1 1.6 copy-done.3
  7.7 5.3 %shard_map.37 = (bf16[2,64,384,128]{3,2,1,0:T(8,128)(2,1)}, bf16[2,64,128,128]{3,2,1,0:T(8,128)(2,1)S(1)}) custom-call(s32[64]{0:T(128)S(1)} %reshape.91.rows_ref, bf16[2,32,384,128]{3,2,1,0:T(8,128)(2,1)S(1)} %copy-done.1, bf16[2,32,128,128]{3,2,1,0:T(8,128)(2,1)S(1)} %copy-done.3), custom_call_target="tpu_custom_call" | custom-call | tf_op jit(solution)/shard_map/pallas_call | solution.py:67
  13.0 0.0 copy-start.2
  13.0 1.9 copy-done.2
  14.9 365.0 %shard_map.38 = (bf16[2,64,384,128]{3,2,1,0:T(8,128)(2,1)}, bf16[2,64,512,128]{3,2,1,0:T(8,128)(2,1)}) custom-call(bf16[2,64,384,128]{3,2,1,0:T(8,128)(2,1)} %get-tuple-element.9.sent_query_ref, bf16[2,64,128,128]{3,2,1,0:T(8,128)(2,1)} %copy-done.2), custom_call_target="tpu_custom_call" | custom-call | tf_op jit(solution)/shard_map/pallas_call | solution.py:193
  380.0 0.0 copy-start
  380.0 4.6 %copy-done = bf16[2,64,384,128]{3,2,1,0:T(8,128)(2,1)S(1)} copy-done((bf16[2,64,384,128]{3,2,1,0:T(8,128)(2,1)S(1)}, bf16[2,64,384,128]{3,2,1,0:T(8,128)(2,1)}, u32[]{:S(2)}) %copy-start) | copy-done | bytes 12582936
  384.5 26.7 %shard_map.39 = bf16[128,384,512]{2,1,0:T(8,128)(2,1)} custom-call(s32[128]{0:T(128)S(1)} %add.41.source_ref, s32[128]{0:T(128)S(1)} %reshape.96.live_ref, bf16[128,384,128]{2,1,0:T(8,128)(2,1)S(1)} %bitcast.3, bf16[128,384,128]{2,1,0:T(8,128)(2,1)S(1)} %bitcast.4, bf16[128,384,128]{2,1,0:T(8,128)(2,1)S(1)} %bitcast.5, bf16[128,384,128]{2,1,0:T(8,128)(2,1)S(1)} %bitcast.6, ...), custom_call_target="tpu_custom_call" | custom-call | tf_op jit(solution)/shard_map/pallas_call | solution.py:233
  (6 shorter events, 0.0 us)
Async XLA Ops:
  3.3 2.8 copy-start.1
  6.1 1.6 copy-start.3
  13.0 1.9 copy-start.2
  380.0 4.6 %copy-start = (bf16[2,64,384,128]{3,2,1,0:T(8,128)(2,1)S(1)}, bf16[2,64,384,128]{3,2,1,0:T(8,128)(2,1)}, u32[]{:S(2)}) copy-start(bf16[2,64,384,128]{3,2,1,0:T(8,128)(2,1)} %get-tuple-element.11) | copy-start | bytes 37748740
